TPU v7x, 256 devices: a whole 4x4x8 slice. The times are simulated.
256 devices in a mesh: seq: 64 (over y, z_hi, x), tp: 4 (over z_lo, core).
Axes of the slice: x: 4, y: 4, z: 8 (z_hi: 4, z_lo: 2; z = z_hi * 2 + z_lo), core: 2. Of those that a mesh axis runs over, the one named last changes fastest.
Arguments:
- tokens: bfloat16 [32256, 4096], P('seq'), may hold values from -6 to 6
- norm_gain: float32 [4096], replicated, may hold values from 0.5 to 1.5
- gate_weight: bfloat16 [4096, 7168], P('seq', 'tp'), may hold values from -0.09375 to 0.09375
- up_weight: bfloat16 [4096, 7168], P('seq', 'tp'), may hold values from -0.09375 to 0.09375
Outputs:
- saved_hidden: bfloat16 [32256, 7168], P('seq', 'tp')
- token_scales: float32 [32256], P('seq')
All inputs are finite; a program needn't handle non-finite values. Where the computation divides by a largest or mean magnitude, that divisor is 1e-20 or more.
Results may differ from a plain program's by a relative error of at most 0.0061.
Values may be sent and summed in bfloat16 or wider, within the bound.
A program may use at most 128 MiB of HBM per device.

v0:
```python
import jax
import jax.numpy as jnp
from jax import lax
from jax.sharding import PartitionSpec as P


def norm_rows(block, norm_gain):
    values = block.astype(jnp.float32)
    mean_square = jnp.mean(values * values, axis=1, keepdims=True)
    return (values * lax.rsqrt(mean_square + 1e-05) * norm_gain[None, :]).astype(jnp.bfloat16)


def add_rows(normed, piece):
    return jnp.dot(normed, piece, preferred_element_type=jnp.float32)


def shards(tokens, norm_gain, gate_weight, up_weight):
    normed = norm_rows(tokens, norm_gain)

    def add_single(piece):
        return add_rows(normed, piece)

    gate = add_single(lax.all_gather(gate_weight, "seq", axis=0, tiled=True))
    up = add_single(lax.all_gather(up_weight, "seq", axis=0, tiled=True))
    hidden = jax.nn.silu(gate) * up
    local_peak = jnp.max(jnp.abs(hidden), axis=1)
    scales = lax.pmax(local_peak, "tp") + 1e-06
    saved = (hidden / scales[:, None]).astype(jnp.bfloat16)
    return (saved, scales)


def solution(mesh):
    in_specs = (P("seq", None), P(), P("seq", "tp"), P("seq", "tp"))
    out_specs = (P("seq", "tp"), P("seq"))
    return jax.shard_map(shards, mesh=mesh, in_specs=in_specs, out_specs=out_specs, check_vma=False)
```

profile of v0, /device:TPU:4, one launch (start us, length us, event | category | flops | bytes accessed | tf_op | source)
XLA Modules:
  0.0 360.7 jit_solution(13655028735498425475)
XLA Ops:
  7.2 0.0 copy-start.1
  7.2 0.0 all-gather.3.cloned.1.call-start
  7.2 0.7 all-gather.3.cloned.1.call-update
  7.9 0.0 all-gather.5.cloned.1.call-start
  8.0 0.7 all-gather.5.cloned.1.call-update
  8.7 3.1 fusion
  11.7 143.4 %all-gather.3.cloned.1.call-done = bf16[4096,1792]{1,0:T(8,128)(2,1)} async-done(((bf16[64,1792]{1,0:T(8,128)(2,1)}), bf16[4096,1792]{1,0:T(8,128)(2,1)}) %all-gather.3.cloned.1.call-update) | async-done | bytes 14680080 | tf_op jit(solution)/shard_map/all_gather | solution.py:23
  155.1 0.0 copy-done.1
  155.1 14.5 %fusion.4 = f32[504,1792]{1,0:T(8,128)} fusion(bf16[4096,1792]{1,0:T(8,128)(2,1)} %all-gather.3.cloned.1.call-done, bf16[504,4096]{1,0:T(8,128)(2,1)} %param.4, f32[4096]{0:T(1024)S(1)} %copy-done.1, f32[504]{0:T(512)S(1)} %add_rsqrt_fusion), kind=kOutput, calls=%fused_computation.8 | convolution fusion | flops 7407009792 | bytes 22439904 | tf_op jit(solution)/shard_map/dot_general | solution.py:14
  169.6 142.6 %all-gather.5.cloned.1.call-done = bf16[4096,1792]{1,0:T(8,128)(2,1)} async-done(((bf16[64,1792]{1,0:T(8,128)(2,1)}), bf16[4096,1792]{1,0:T(8,128)(2,1)}) %all-gather.5.cloned.1.call-update) | async-done | bytes 14680080 | tf_op jit(solution)/shard_map/all_gather | solution.py:24
  312.3 16.1 %abs_reduce_fusion = (f32[504]{0:T(512)S(1)}, f32[504,1792]{1,0:T(8,128)}) fusion(bf16[4096,1792]{1,0:T(8,128)(2,1)} %all-gather.5.cloned.1.call-done, bf16[504,4096]{1,0:T(8,128)(2,1)} %param.4, f32[4096]{0:T(1024)S(1)} %copy-done.1, f32[504]{0:T(512)S(1)} %add_rsqrt_fusion, f32[504,1792]{1,0:T(8,128)} %fusion.4), kind=kOutput, calls=%fused_computation.6 | convolution fusion | flops 7413331456 | bytes 26054592 | tf_op jit(solution)/shard_map/dot_general | solution.py:14
  328.4 21.8 %pmax.7 = f32[504]{0:T(512)S(1)} all-reduce(f32[504]{0:T(512)S(1)} %get-tuple-element.2), channel_id=1, replica_groups=mesh['seq'=64,'tp'=4] {'tp'}, use_global_device_ids=true, to_apply=%region_2.3 | all-reduce | flops 504 | bytes 4032 | tf_op jit(solution)/shard_map/pmax | solution.py:27
  350.2 0.0 copy-start
  350.2 3.6 %divide_convert_fusion = bf16[504,1792]{1,0:T(8,128)(2,1)} fusion(f32[504,1792]{1,0:T(8,128)} %get-tuple-element.3, f32[504]{0:T(512)S(1)} %broadcast_add_fusion), kind=kLoop, calls=%fused_computation.5 | loop fusion | flops 1806336 | bytes 5421024 | tf_op jit(solution)/shard_map/convert_element_type | solution.py:28
  353.8 0.0 copy-done
  (2 shorter events, 0.0 us)
Async XLA Ops:
  7.2 147.9 %copy-start.1 = (f32[4096]{0:T(1024)S(1)}, f32[4096]{0:T(1024)}, u32[]{:S(2)}) copy-start(f32[4096]{0:T(1024)} %param.5) | copy-start | bytes 49156
  7.2 147.9 %all-gather.3.cloned.1.call-start = ((), (), s32[]{:S(2)}) async-start(), calls=%async_computation | async-start | bytes 14909440 | tf_op jit(solution)/shard_map/all_gather | solution.py:23
  7.9 304.4 %all-gather.5.cloned.1.call-start = ((), (), s32[]{:S(2)}) async-start(), calls=%async_computation.1 | async-start | bytes 14909440 | tf_op jit(solution)/shard_map/all_gather | solution.py:24
  350.2 3.6 %copy-start = (f32[504]{0:T(512)}, f32[504]{0:T(512)S(1)}, u32[]{:S(2)}) copy-start(f32[504]{0:T(512)S(1)} %broadcast_add_fusion) | copy-start | bytes 6052
Sparse Core Ops, SparseCore 0:
  11.3 143.7 all-gather.2
  158.4 153.8 all-gather.4
where the time goes:
time: 361 us
  waiting for transfers between devices  287 us (80%)
  matrix products  30.6 us (8%)
  blocking collectives  21.8 us (6%)
  between operations  14 us (4%)
  other arithmetic  6.69 us (2%)
    all_gather x1, waiting for transfers between devices, shards(): gate = add_single(lax.all_gather(gate_weight, 'seq', axis=0, tiled=True))  143 us
    all_gather x1, waiting for transfers between devices, shards(): up = add_single(lax.all_gather(up_weight, 'seq', axis=0, tiled=True))  143 us
    dot_general x2, matrix products, add_rows(): return jnp.dot(normed, piece, preferred_element_type=jnp.float32)  30.6 us
    pmax x1, blocking collectives, shards(): scales = lax.pmax(local_peak, 'tp') + 1e-06  21.8 us
  transfers between devices with their start and end apart: 2, of which 2 were waited for; matrix products, arithmetic and copies ran while one was open for 5% of the time, Pallas kernels for 0%

commit v1 on v0

--- a/solution.py
+++ b/solution.py
@@ -2,6 +2,13 @@
 import jax.numpy as jnp
 from jax import lax
 from jax.sharding import PartitionSpec as P
+
+
+def swapped_in(value, name, along):
+    peers = lax.axis_size(name)
+    shards = jnp.stack([value for _ in range(peers)])
+    shards = lax.all_to_all(shards, name, split_axis=0, concat_axis=0)
+    return jnp.concatenate(shards, axis=along)
 
 
 def norm_rows(block, norm_gain):
@@ -21,7 +28,7 @@
         return add_rows(normed, piece)
 
     gate = add_single(lax.all_gather(gate_weight, "seq", axis=0, tiled=True))
-    up = add_single(lax.all_gather(up_weight, "seq", axis=0, tiled=True))
+    up = add_single(swapped_in(up_weight, "seq", 0))
     hidden = jax.nn.silu(gate) * up
     local_peak = jnp.max(jnp.abs(hidden), axis=1)
     scales = lax.pmax(local_peak, "tp") + 1e-06

time: 361 us -> 505 us (1.40)
  waiting for transfers between devices: 287 us -> 410 us
  starting transfers between devices: 0.08 us -> 14.8 us
  local copies, waits for them, and re-layouts: 0.01 us -> 7.95 us
    all_gather x1, waiting for transfers between devices: 143 us -> 391 us  [shards(): gate = add_single(lax.all_gather(gate_weight, 'seq', axis=0, tiled=True))]
    all_gather x1 -> x0, waiting for transfers between devices: 143 us -> none  [shards(): up = add_single(lax.all_gather(up_weight, 'seq', axis=0, tiled=True))]
    all_to_all x0 -> x1, waiting for transfers between devices: none -> 18.1 us  [swapped_in(): shards = lax.all_to_all(shards, name, split_axis=0, concat_axis=0)]
    all_to_all x0 -> x1, starting transfers between devices: none -> 14.8 us  [swapped_in(): shards = lax.all_to_all(shards, name, split_axis=0, concat_axis=0)]
    another operation x0 -> x1, local copies, waits for them, and re-layouts: none -> 7.94 us  [swapped_in(): shards = jnp.stack([value for _ in range(peers)])]
where the time goes in v1:
time: 505 us
  waiting for transfers between devices  410 us (81%)
  matrix products  30.7 us (6%)
  blocking collectives  20.2 us (4%)
  starting transfers between devices  14.8 us (3%)
  between operations  14 us (3%)
  local copies, waits for them, and re-layouts  7.95 us (2%)
  other arithmetic  6.7 us (1%)
    all_gather x1, waiting for transfers between devices, shards(): gate = add_single(lax.all_gather(gate_weight, 'seq', axis=0, tiled=True))  391 us
    dot_general x2, matrix products, add_rows(): return jnp.dot(normed, piece, preferred_element_type=jnp.float32)  30.7 us
    pmax x1, blocking collectives, shards(): scales = lax.pmax(local_peak, 'tp') + 1e-06  20.2 us
    all_to_all x1, waiting for transfers between devices, swapped_in(): shards = lax.all_to_all(shards, name, split_axis=0, concat_axis=0)  18.1 us
    all_to_all x1, starting transfers between devices, swapped_in(): shards = lax.all_to_all(shards, name, split_axis=0, concat_axis=0)  14.8 us
  transfers between devices with their start and end apart: 2, of which 2 were waited for; matrix products, arithmetic and copies ran while one was open for 5% of the time, Pallas kernels for 0%

profile of v1, /device:TPU:4, one launch (start us, length us, event | category | flops | bytes accessed | tf_op | source)
XLA Modules:
  0.0 504.7 jit_solution(9573004872556881066)
XLA Ops:
  7.2 0.0 all-gather.2.cloned.1.call-start
  7.2 0.7 all-gather.2.cloned.1.call-update
  7.9 7.9 %stack.2 = bf16[64,64,1792]{2,1,0:T(8,128)(2,1)} broadcast(bf16[64,1792]{1,0:T(8,128)(2,1)} %param.7), dimensions={1,2} | broadcast | bytes 14909440 | tf_op jit(solution)/shard_map/stack | solution.py:9
  15.8 14.8 %all-to-all-start = ((bf16[64,64,1792]{2,1,0:T(8,128)(2,1)}), bf16[64,64,1792]{2,1,0:T(8,128)(2,1)}, u32[]{:S(2)}, u32[]{:S(2)}) async-start(bf16[64,64,1792]{2,1,0:T(8,128)(2,1)} %stack.2), calls=%async_computation | async-start | bytes 29360128 | tf_op jit(solution)/shard_map/all_to_all | solution.py:10
  30.6 0.0 copy-start.1
  30.6 3.1 fusion
  33.7 391.4 %all-gather.2.cloned.1.call-done = bf16[4096,1792]{1,0:T(8,128)(2,1)} async-done(((bf16[64,1792]{1,0:T(8,128)(2,1)}), bf16[4096,1792]{1,0:T(8,128)(2,1)}) %all-gather.2.cloned.1.call-update) | async-done | bytes 14680080 | tf_op jit(solution)/shard_map/all_gather | solution.py:30
  425.1 0.0 copy-done.1
  425.1 14.6 %fusion.4 = f32[504,1792]{1,0:T(8,128)} fusion(bf16[4096,1792]{1,0:T(8,128)(2,1)} %all-gather.2.cloned.1.call-done, bf16[504,4096]{1,0:T(8,128)(2,1)} %param.4, f32[4096]{0:T(1024)S(1)} %copy-done.1, f32[504]{0:T(512)S(1)} %add_rsqrt_fusion), kind=kOutput, calls=%fused_computation.8 | convolution fusion | flops 7407009792 | bytes 22439904 | tf_op jit(solution)/shard_map/dot_general | solution.py:21
  439.7 18.1 %all-to-all-done = bf16[64,64,1792]{2,1,0:T(8,128)(2,1)} async-done(((bf16[64,64,1792]{2,1,0:T(8,128)(2,1)}), bf16[64,64,1792]{2,1,0:T(8,128)(2,1)}, u32[]{:S(2)}, u32[]{:S(2)}) %all-to-all-start) | async-done | bytes 14680096 | tf_op jit(solution)/shard_map/all_to_all | solution.py:10
  457.8 16.1 %abs_reduce_fusion = (f32[504]{0:T(512)S(1)}, f32[504,1792]{1,0:T(8,128)}) fusion(bf16[4096,1792]{1,0:T(8,128)(2,1)} %bitcast, bf16[504,4096]{1,0:T(8,128)(2,1)} %param.4, f32[4096]{0:T(1024)S(1)} %copy-done.1, f32[504]{0:T(512)S(1)} %add_rsqrt_fusion, f32[504,1792]{1,0:T(8,128)} %fusion.4), kind=kOutput, calls=%fused_computation.6 | convolution fusion | flops 7413331456 | bytes 26054592 | tf_op jit(solution)/shard_map/dot_general | solution.py:21
  473.9 20.2 %pmax.7 = f32[504]{0:T(512)S(1)} all-reduce(f32[504]{0:T(512)S(1)} %get-tuple-element.2), channel_id=1, replica_groups=mesh['seq'=64,'tp'=4] {'tp'}, use_global_device_ids=true, to_apply=%region_2.3 | all-reduce | flops 504 | bytes 4032 | tf_op jit(solution)/shard_map/pmax | solution.py:34
  494.2 0.0 copy-start
  494.2 3.6 divide_convert_fusion
  497.8 0.0 copy-done
  (2 shorter events, 0.0 us)
Async XLA Ops:
  7.2 417.9 %all-gather.2.cloned.1.call-start = ((), (), s32[]{:S(2)}) async-start(), calls=%async_computation.1 | async-start | bytes 14909440 | tf_op jit(solution)/shard_map/all_gather | solution.py:30
  15.8 442.0 %all-to-all-start = ((bf16[64,64,1792]{2,1,0:T(8,128)(2,1)}), bf16[64,64,1792]{2,1,0:T(8,128)(2,1)}, u32[]{:S(2)}, u32[]{:S(2)}) async-start(bf16[64,64,1792]{2,1,0:T(8,128)(2,1)} %stack.2), calls=%async_computation | async-start | bytes 29360128 | tf_op jit(solution)/shard_map/all_to_all | solution.py:10
  30.6 394.5 %copy-start.1 = (f32[4096]{0:T(1024)S(1)}, f32[4096]{0:T(1024)}, u32[]{:S(2)}) copy-start(f32[4096]{0:T(1024)} %param.5) | copy-start | bytes 49156
  494.2 3.6 copy-start
Sparse Core Ops, SparseCore 0:
  11.3 413.7 all-gather.1
